TPU v7x, 32 devices: a whole 2x2x4 slice. The times are simulated.
32 devices in a mesh: chan: 8 (over y, x, core), win: 4 (over z).
Axes of the slice: x: 2, y: 2, z: 4, core: 2. Of those that a mesh axis runs over, the one named last changes fastest.
Arguments:
- records: bfloat16 [4, 128, 7680], P('win', 'chan'), may hold values from -6 to 6
- source_rows: int32 [1, 256], replicated, may hold values from 0 to 15
Outputs:
- correlation: float32 [256, 128, 2048], P(None, ('chan', 'win'))
Inputs may be any that keep to these rules, and one draw needn't show every extreme that they name: Entry j of row b of source_rows names a channel of channel shard j // 32, counted within that shard; entries may repeat.
All inputs are finite; a program needn't handle non-finite values.
Results may differ from a plain program's by a relative error of at most 0.0063.
Values may be sent and summed in bfloat16 or wider, within the bound.
A program may use at most 64 MiB of HBM per device.

v0:
```python
import math

import jax
import jax.numpy as jnp
from jax import lax
from jax.sharding import PartitionSpec as P

S = 7680
NBINS = 512
HALF = 32
FIRST_BIN = 64
MAXLAG = 1024


full_turn = 2.0 * math.pi


def band_table():
    bin_ids = FIRST_BIN - HALF + jnp.arange(NBINS + 2 * HALF, dtype=jnp.int32)
    sample_ids = jnp.arange(S, dtype=jnp.int32)
    angles = (sample_ids[:, None] * bin_ids[None, :] % S).astype(jnp.float32) * (full_turn / S)
    return jnp.concatenate([jnp.cos(angles), -jnp.sin(angles)], axis=1).astype(jnp.bfloat16)


def lag_weights():
    bin_ids = FIRST_BIN + jnp.arange(NBINS, dtype=jnp.int32)
    lag_ids = jnp.arange(2 * MAXLAG, dtype=jnp.int32) - MAXLAG
    angles = (bin_ids[:, None] * lag_ids[None, :] % S).astype(jnp.float32) * (full_turn / S)
    return jnp.concatenate([jnp.cos(angles), -jnp.sin(angles)], axis=0).astype(jnp.bfloat16)


def normalize(spectrum):
    extent = NBINS + 2 * HALF
    real_part = spectrum[:, :extent]
    imag_part = spectrum[:, extent:]
    magnitude = jnp.sqrt(real_part * real_part + imag_part * imag_part)
    smooth = magnitude[:, 0:NBINS]
    for offset in range(1, 2 * HALF + 1):
        smooth = smooth + magnitude[:, offset : offset + NBINS]
    smooth = smooth / (2 * HALF + 1) + 1e-06
    centre_re = real_part[:, HALF : HALF + NBINS] / smooth
    centre_im = imag_part[:, HALF : HALF + NBINS] / smooth
    return jnp.stack([centre_re, centre_im], axis=1).astype(jnp.bfloat16)


def whiten(row_data):
    return normalize(jnp.dot(row_data, band_table(), preferred_element_type=jnp.float32))


def cross_terms(source_part, receiver_part):
    real_sum = jnp.einsum(
        "wbi,wri->bri",
        source_part[:, :, 0],
        receiver_part[:, :, 0],
        preferred_element_type=jnp.float32,
    ) + jnp.einsum(
        "wbi,wri->bri",
        source_part[:, :, 1],
        receiver_part[:, :, 1],
        preferred_element_type=jnp.float32,
    )
    imag_sum = jnp.einsum(
        "wbi,wri->bri",
        source_part[:, :, 1],
        receiver_part[:, :, 0],
        preferred_element_type=jnp.float32,
    ) - jnp.einsum(
        "wbi,wri->bri",
        source_part[:, :, 0],
        receiver_part[:, :, 1],
        preferred_element_type=jnp.float32,
    )
    return jnp.stack([real_sum, imag_sum], axis=2)


def transform(spectra, weights, lag_scale):
    count_src, count_rec = (spectra.shape[0], spectra.shape[1])
    rounded = spectra.astype(jnp.bfloat16).reshape(count_src * count_rec, 2 * NBINS)
    result = jnp.dot(rounded, weights, preferred_element_type=jnp.float32) * lag_scale
    return result.reshape(count_src, count_rec, 2 * MAXLAG)


def collect(portion):
    portion = lax.all_gather(portion, "win", axis=0, tiled=True)
    return lax.all_gather(portion, "chan", axis=1, tiled=True)


def per_device(records, source_rows):
    windows_here, rows_here, samples = records.shape
    whitened = whiten(records.reshape(windows_here * rows_here, samples)).reshape(
        windows_here, rows_here, 2, NBINS
    )
    shards = lax.axis_size("chan")
    block_len = source_rows.shape[1]
    per_shard = block_len // shards
    weights = lag_weights()
    lag_scale = math.sqrt(2.0 / (lax.axis_size("win") * windows_here * NBINS))
    receivers = lax.all_to_all(whitened, "win", split_axis=1, concat_axis=0, tiled=True)
    everything = collect(whitened)
    base_rows = jnp.arange(block_len, dtype=jnp.int32) // per_shard * rows_here
    chosen_rows = source_rows[0]
    source_block = jnp.take(everything, base_rows + chosen_rows, axis=1)
    spectra = cross_terms(source_block, receivers)
    results = transform(spectra, weights, lag_scale)
    return results


def solution(mesh):
    in_specs = (P("win", "chan", None), P())
    out_specs = P(None, ("chan", "win"), None)
    return jax.shard_map(
        per_device, mesh=mesh, in_specs=in_specs, out_specs=out_specs, check_vma=False
    )
```

profile of v0, /device:TPU:0, one launch (start us, length us, event | category | flops | bytes accessed | tf_op | source)
XLA Modules:
  0.0 173.3 jit_solution(13468943092286466024)
XLA Ops:
  6.5 0.0 copy-start
  6.5 0.0 all-gather.2.cloned.1.call-start
  6.5 74.1 %cosine_convert_fusion = (bf16[7680,576]{0,1:T(8,128)(2,1)S(1)}, bf16[7680,576]{0,1:T(8,128)(2,1)S(1)}) fusion(s32[576]{0:T(1024)S(1)} %iota_add_fusion.1), kind=kLoop, calls=%fused_computation.9 | loop fusion | flops 53084160 | bytes 17697024 | tf_op jit(solution)/shard_map/convert.12
  80.6 0.0 copy-done
  80.6 0.0 copy-start.3
  80.6 4.6 %fusion.17 = f32[16,1152]{1,0:T(8,128)S(1)} fusion(bf16[7680,576]{0,1:T(8,128)(2,1)S(1)} %get-tuple-element.12, bf16[7680,576]{0,1:T(8,128)(2,1)S(1)} %get-tuple-element.11, bf16[1,16,7680]{2,1,0:T(8,128)(2,1)S(1)} %copy-done), kind=kOutput, calls=%fused_computation.27 | convolution fusion | flops 318504960 | bytes 18014208 | tf_op jit(solution)/shard_map/dot_general | solution.py:47
  85.3 0.1 fusion.30
  85.4 0.6 fusion.35
  86.0 0.1 fusion.36
  86.1 15.1 %all_gather.6 = bf16[4,16,2,512]{3,1,2,0:T(8,128)(2,1)S(1)} all-gather(bf16[1,16,2,512]{3,1,2,0:T(8,128)(2,1)S(1)} %pad_maximum_fusion.1), channel_id=1, replica_groups=mesh['chan'=8,'win'=4] {'win'}, dimensions={0}, use_global_device_ids=true | all-gather | bytes 163840 | tf_op jit(solution)/shard_map/all_gather | solution.py:84
  101.2 0.8 copy.32
  101.9 0.0 all-gather.2.cloned.1.call-update
  102.0 0.6 copy.30
  102.6 5.0 %all-to-all-start = ((bf16[1,16,2,512]{3,2,0,1:T(2,128)(2,1)}), bf16[1,16,2,512]{3,2,0,1:T(2,128)(2,1)S(1)}, u32[]{:S(2)}, u32[]{:S(2)}) async-start(bf16[1,16,2,512]{3,2,0,1:T(2,128)(2,1)} %copy.30), calls=%async_computation | async-start | bytes 65536 | tf_op jit(solution)/shard_map/all_to_all | solution.py:98
  107.6 0.0 copy-done.3
  107.6 19.4 %cosine_convert_fusion.1 = (bf16[512,2048]{1,0:T(8,128)(2,1)}, bf16[512,2048]{1,0:T(8,128)(2,1)}) fusion(s32[2048]{0:T(1024)S(1)} %iota_add_fusion, s32[512]{0:T(512)S(1)} %iota_add_fusion.2), kind=kLoop, calls=%fused_computation.22 | loop fusion | flops 12582912 | bytes 4204544 | tf_op jit(solution)/shard_map/convert
  127.0 0.0 all-to-all-done
  127.1 0.1 fusion.44
  127.1 0.4 copy.36
  127.5 0.4 copy.37
  127.8 0.0 all-gather.2.cloned.1.call-done
  127.9 3.7 %gather_fusion = bf16[256,4,2,512]{3,1,2,0:T(4,128)(2,1)S(1)} fusion(bf16[4,128,2,512]{3,0,2,1:T(4,128)(2,1)} %all-gather.2.cloned.1.call-done, s32[1024]{0:T(1024)S(1)} %pad_clamp_fusion), kind=kCustom, calls=%fused_computation | custom fusion | bytes 4195328 | tf_op jit(solution)/shard_map/jit(_take)/gather | solution.py:102
  131.6 4.3 %copy.33 = bf16[256,4,2,512]{0,1,3,2:T(4,128)(2,1)} copy(bf16[256,4,2,512]{3,1,2,0:T(4,128)(2,1)S(1)} %gather_fusion) | data formatting | bytes 4194304 | tf_op jit(solution)/shard_map/jit(_take)/gather | solution.py:102
  135.8 2.5 %select_bitcast_fusion = bf16[4,256,2,512]{1,0,3,2:T(4,128)(2,1)S(1)} fusion(bf16[256,4,2,512]{0,1,3,2:T(4,128)(2,1)} %copy.33, pred[256]{0:T(512)(128)(4,1)S(1)} %compare_and_fusion), kind=kLoop, calls=%fused_computation.29 | loop fusion | flops 1048576 | bytes 4194560 | tf_op jit(solution)/shard_map/jit(_take)/select_n | solution.py:102
  138.3 0.7 fusion.22
  139.0 0.7 fusion.23
  139.7 0.8 fusion.20
  140.5 0.8 fusion.21
  141.4 1.5 pad_maximum_fusion
  142.9 4.3 %copy.35 = bf16[256,4,2,512]{3,2,1,0:T(2,128)(2,1)} copy(bf16[256,4,2,512]{0,1,3,2:T(4,128)(2,1)S(1)} %pad_maximum_fusion) | data formatting | bytes 4194304 | tf_op jit(solution)/shard_map/stack | solution.py:73
  147.1 0.0 copy-start.1
  147.1 0.0 copy-start.2
  147.1 2.3 %copy.38 = bf16[128,8,2,512]{3,1,2,0:T(8,128)(2,1)S(1)} copy(bf16[128,8,2,512]{3,2,1,0:T(2,128)(2,1)} %bitcast.46) | data formatting | bytes 4194304
  149.4 0.0 copy-done.1
  149.4 0.5 copy-done.2
  150.0 6.8 %convolution_multiply_fusion = f32[1024,2048]{1,0:T(8,128)} fusion(bf16[1024,1024]{1,0:T(8,128)(2,1)S(1)} %bitcast.47, bf16[512,2048]{1,0:T(8,128)(2,1)S(1)} %copy-done.2, bf16[512,2048]{1,0:T(8,128)(2,1)S(1)} %copy-done.1), kind=kOutput, calls=%fused_computation.15 | convolution fusion | flops 4305453056 | bytes 14680064 | tf_op jit(solution)/shard_map/dot_general | solution.py:79
  156.7 9.7 %reshape.122 = f32[256,4,2048]{2,1,0:T(4,128)} reshape(f32[1024,2048]{1,0:T(8,128)} %convolution_multiply_fusion) | data formatting | bytes 16777216 | tf_op jit(solution)/shard_map/reshape | solution.py:80
  (7 shorter events, 0.0 us)
Async XLA Ops:
  6.5 74.1 %copy-start = (bf16[1,16,7680]{2,1,0:T(8,128)(2,1)S(1)}, bf16[1,16,7680]{2,1,0:T(8,128)(2,1)}, u32[]{:S(2)}) copy-start(bf16[1,16,7680]{2,1,0:T(8,128)(2,1)} %param.2) | copy-start | bytes 737284
  6.5 121.3 %all-gather.2.cloned.1.call-start = ((), (), s32[]{:S(2)}) async-start(), calls=%async_computation.1 | async-start | bytes 1179648 | tf_op jit(solution)/shard_map/all_gather | solution.py:85
  80.6 27.0 %copy-start.3 = (s32[1,256]{1,0:T(1,128)S(1)}, s32[1,256]{1,0:T(1,128)}, u32[]{:S(2)}) copy-start(s32[1,256]{1,0:T(1,128)} %param.3) | copy-start | bytes 3076
  102.6 24.4 %all-to-all-start = ((bf16[1,16,2,512]{3,2,0,1:T(2,128)(2,1)}), bf16[1,16,2,512]{3,2,0,1:T(2,128)(2,1)S(1)}, u32[]{:S(2)}, u32[]{:S(2)}) async-start(bf16[1,16,2,512]{3,2,0,1:T(2,128)(2,1)} %copy.30), calls=%async_computation | async-start | bytes 65536 | tf_op jit(solution)/shard_map/all_to_all | solution.py:98
  147.1 2.3 %copy-start.1 = (bf16[512,2048]{1,0:T(8,128)(2,1)S(1)}, bf16[512,2048]{1,0:T(8,128)(2,1)}, u32[]{:S(2)}) copy-start(bf16[512,2048]{1,0:T(8,128)(2,1)} %get-tuple-element.9) | copy-start | bytes 6291460
  147.1 2.9 %copy-start.2 = (bf16[512,2048]{1,0:T(8,128)(2,1)S(1)}, bf16[512,2048]{1,0:T(8,128)(2,1)}, u32[]{:S(2)}) copy-start(bf16[512,2048]{1,0:T(8,128)(2,1)} %get-tuple-element.10) | copy-start | bytes 6291460
Sparse Core Ops, SparseCore 0:
  102.1 25.0 all-gather.1
where the time goes:
time: 174 us; the launch traced here: 173 us
  other arithmetic  98.3 us (56%)
  local copies, waits for them, and re-layouts  27 us (16%)
  blocking collectives  15.1 us (9%)
  matrix products  14.4 us (8%)
  between operations  13.6 us (8%)
  starting transfers between devices  4.97 us (3%)
    another operation x2, other arithmetic  93.5 us
    all_gather x1, blocking collectives, collect(): portion = lax.all_gather(portion, 'win', axis=0, tiled=True)  15.1 us
    reshape x1, local copies, waits for them, and re-layouts, transform(): return result.reshape(count_src, count_rec, 2 * MAXLAG)  9.75 us
    gather x2, local copies, waits for them, and re-layouts, per_device(): source_block = jnp.take(everything, base_rows + chosen_rows, axis=1)  7.95 us
    dot_general x1, matrix products, transform(): jnp.dot(rounded, weights, preferred_element_type=jnp.float32) * lag_scale  6.77 us
    all_to_all x1, starting transfers between devices, per_device(): lax.all_to_all(whitened, 'win', split_axis=1, concat_axis=0, tiled=True)  4.97 us
    dot_general x1, matrix products, whiten(): jnp.dot(row_data, band_table(), preferred_element_type=jnp.float32)  4.64 us
    another operation x1, local copies, waits for them, and re-layouts, cross_terms(): return jnp.stack([real_sum, imag_sum], axis=2)  4.26 us
  transfers between devices with their start and end apart: 2, of which 0 were waited for; matrix products, arithmetic and copies ran while one was open for 12% of the time, Pallas kernels for 0%

commit v1 on v0

v1 whole, which is shorter than its diff:
```python
import functools
import math

import jax
import jax.numpy as jnp
import ml_dtypes
import numpy as np
from jax import lax
from jax.experimental import pallas as pl
from jax.experimental.pallas import tpu as pltpu
from jax.sharding import PartitionSpec as P

S = 7680
NBINS = 512
HALF = 32
FIRST_BIN = 64
MAXLAG = 1024

INNER = 512
OUTER = S // INNER
LOW = FIRST_BIN - HALF
WIDE = 640
CB = 64
LANES = 128
GROUPS = 2 * MAXLAG // LANES
MESH = pl.DeviceIdType.MESH
bf16 = jnp.bfloat16
f32 = jnp.float32


def angles(left, right):
    turn = np.float32(2.0 * math.pi / S)
    return (left[:, None] * right[None, :] % S).astype(np.float32) * turn


def inner_table():
    a = angles(np.arange(INNER), LOW + np.arange(WIDE))
    return np.concatenate([np.cos(a), -np.sin(a)], axis=1).astype(ml_dtypes.bfloat16)


def outer_table():
    a = angles(INNER * np.arange(OUTER), LOW + np.arange(WIDE))
    return np.stack([np.cos(a), np.sin(a)]).astype(np.float32)


def lag_table():
    a = angles(FIRST_BIN + np.arange(NBINS), np.arange(2 * MAXLAG) - MAXLAG)
    return np.concatenate([np.cos(a), -np.sin(a)], axis=0).astype(ml_dtypes.bfloat16)


def spectra_of(x_ref, table_ref, outer_ref):
    rows = x_ref.shape[0]
    parts = [x_ref[:, i * INNER : (i + 1) * INNER] for i in range(OUTER)]
    z = jnp.dot(
        jnp.concatenate(parts, axis=0), table_ref[...], preferred_element_type=f32
    )
    re = im = None
    for i in range(OUTER):
        zr = z[i * rows : (i + 1) * rows, :WIDE]
        zi = z[i * rows : (i + 1) * rows, WIDE:]
        c = outer_ref[0, i : i + 1, :]
        s = outer_ref[1, i : i + 1, :]
        tr = zr * c + zi * s
        ti = zi * c - zr * s
        re = tr if re is None else re + tr
        im = ti if im is None else im + ti
    return re, im


def whiten(re, im):
    total = jnp.sqrt(re * re + im * im)
    first = total
    span = 1
    while span < 2 * HALF:
        total = total + pltpu.roll(total, WIDE - span, 1)
        span *= 2
    total = total + pltpu.roll(first, WIDE - span, 1)
    amplitude = total[:, :NBINS] / (2 * HALF + 1) + 1e-06
    re = pltpu.roll(re, WIDE - HALF, 1)[:, :NBINS] / amplitude
    im = pltpu.roll(im, WIDE - HALF, 1)[:, :NBINS] / amplitude
    return re.astype(bf16), im.astype(bf16)


def gather_kernel(
    n_win, n_chan, x_ref, table_ref, outer_ref, all_ref, s1, r1, s2, r2, s3, r3
):
    rows = x_ref.shape[0]
    chips = n_chan // 2
    win, chan = lax.axis_index("win"), lax.axis_index("chan")
    chip, core = chan // 2, chan % 2
    sibling = chip * 2 + (1 - core)

    def turn(d):
        return lax.rem(win + d, n_win)

    def peer(p):
        return lax.rem(chip + p, chips) * 2 + core

    barrier = pltpu.get_barrier_semaphore()
    friends = [(chan, turn(d)) for d in range(1, n_win)]
    friends += [(peer(p), win) for p in range(1, chips)] + [(sibling, win)]
    for c, w in friends:
        pl.semaphore_signal(
            barrier, inc=1, device_id={"chan": c, "win": w}, device_id_type=MESH
        )

    re, im = whiten(*spectra_of(x_ref, table_ref, outer_ref))
    mine = pl.ds(pl.multiple_of(chan * rows, rows), rows)
    all_ref[win, mine, :NBINS] = re
    all_ref[win, mine, NBINS:] = im
    pl.semaphore_wait(barrier, len(friends))

    def copy(w, c, to_c, to_w, send, recv):
        block = all_ref.at[w, pl.ds(pl.multiple_of(c * rows, rows), rows)]
        return pltpu.make_async_remote_copy(
            src_ref=block,
            dst_ref=block,
            send_sem=send,
            recv_sem=recv,
            device_id={"chan": to_c, "win": to_w},
            device_id_type=MESH,
        )

    along_win = [
        copy(win, chan, chan, turn(d), s1.at[d], r1.at[d]) for d in range(1, n_win)
    ]
    for c in along_win:
        c.start()
    across, to_sibling = {}, {}
    for d in range(n_win):
        w = turn(n_win - d)
        if d:
            copy(w, chan, chan, turn(d), s1.at[d], r1.at[d]).wait_recv()
        for p in range(1, chips):
            across[d, p] = copy(w, chan, peer(p), win, s2.at[d, p], r2.at[d, p])
            across[d, p].start()
        to_sibling[d, 0] = copy(w, chan, sibling, win, s3.at[d, 0], r3.at[d, 0])
        to_sibling[d, 0].start()
    for d in range(n_win):
        w = turn(n_win - d)
        for p in range(1, chips):
            c = peer(chips - p)
            copy(w, c, peer(p), win, s2.at[d, p], r2.at[d, p]).wait_recv()
            to_sibling[d, p] = copy(w, c, sibling, win, s3.at[d, p], r3.at[d, p])
            to_sibling[d, p].start()
    for d in range(n_win):
        w = turn(n_win - d)
        for p in range(chips):
            c = lax.rem(chip + chips - p, chips) * 2 + (1 - core)
            copy(w, c, sibling, win, s3.at[d, p], r3.at[d, p]).wait_recv()
    for c in along_win + list(across.values()) + list(to_sibling.values()):
        c.wait_send()


def gathered(records, n_win, n_chan):
    rows = records.shape[0]
    chips = n_chan // 2
    vmem = pl.BlockSpec(memory_space=pltpu.VMEM)
    dma = pltpu.SemaphoreType.DMA
    return pl.pallas_call(
        functools.partial(gather_kernel, n_win, n_chan),
        out_shape=jax.ShapeDtypeStruct((n_win, n_chan * rows, 2 * NBINS), bf16),
        in_specs=[vmem] * 3,
        out_specs=vmem,
        scratch_shapes=[dma((n_win,))] * 2 + [dma((n_win, chips))] * 4,
        compiler_params=pltpu.CompilerParams(
            collective_id=0, has_side_effects=True, vmem_limit_bytes=40 * 2**20
        ),
        name="gather_spectra",
    )(records, jnp.asarray(inner_table()), jnp.asarray(outer_table()))


def stack_kernel(
    rows, per_shard, scale, all_ref, lag_ref, src_ref, out_ref, own, wide, lhs, corr, sem
):
    n_win, channels, _ = all_ref.shape
    n_rec = rows // n_win
    blocks = channels // CB
    sources = CB // rows * per_shard
    size = CB * GROUPS * n_rec
    lines = GROUPS * n_rec
    chan, win = lax.axis_index("chan"), lax.axis_index("win")
    for w in range(n_win):
        own[w] = all_ref[w, pl.ds(pl.multiple_of(chan * rows, rows), rows), :].astype(f32)
    for w in range(n_win):
        for r in range(n_rec):
            line = own[w, pl.ds(win * n_rec + r, 1), :]
            wide[w, r] = jnp.broadcast_to(line, (16, 2 * NBINS))

    def finish(slot):
        part = out_ref.at[pl.ds(0, sources * lines)]
        pltpu.make_async_copy(part, part, sem.at[slot]).wait()

    @pl.loop(0, blocks)
    def _(b):
        slot = lax.rem(b, 2)

        @pl.when(b >= 2)
        def _():
            finish(slot)

        for k in range(NBINS // LANES):
            at_re = pl.ds(k * LANES, LANES)
            at_im = pl.ds(NBINS + k * LANES, LANES)

            @pl.loop(0, CB // 16)
            def _(i):
                here = pl.ds(pl.multiple_of(b * CB + i * 16, 16), 16)
                s_re = [all_ref[w, here, at_re].astype(f32) for w in range(n_win)]
                s_im = [all_ref[w, here, at_im].astype(f32) for w in range(n_win)]
                for r in range(n_rec):
                    re = im = None
                    for w in range(n_win):
                        r_re, r_im = wide[w, r, :, at_re], wide[w, r, :, at_im]
                        a = s_re[w] * r_re + s_im[w] * r_im
                        c = s_im[w] * r_re - s_re[w] * r_im
                        re = a if re is None else re + a
                        im = c if im is None else im + c
                    to = pl.ds(pl.multiple_of(r * CB + i * 16, 16), 16)
                    lhs[to, at_re] = re.astype(bf16)
                    lhs[to, at_im] = im.astype(bf16)

        for n in range(GROUPS // 2):
            res = jnp.dot(
                lhs[...], lag_ref[:, n * 256 : (n + 1) * 256], preferred_element_type=f32
            )
            res = res * scale
            for h in range(2):
                for r in range(n_rec):
                    for c in range(0, CB, 8):
                        first = slot * size + (c * lines + (2 * n + h) * n_rec + r)
                        corr[pl.ds(first, 8, stride=lines), :] = res[
                            r * CB + c : r * CB + c + 8, h * LANES : (h + 1) * LANES
                        ]

        @pl.loop(0, sources)
        def _(i):
            j = b * sources + i
            c = i // per_shard * rows + src_ref[0, j]
            pltpu.make_async_copy(
                corr.at[pl.ds(pl.multiple_of(slot * size + c * lines, lines), lines)],
                out_ref.at[pl.ds(pl.multiple_of(j * lines, lines), lines)],
                sem.at[slot],
            ).start()

    for b in range(max(0, blocks - 2), blocks):
        finish(b % 2)


def stacked(everything, source_rows, rows, n_chan):
    n_win, channels, _ = everything.shape
    n_rec = rows // n_win
    count = source_rows.shape[1]
    scale = math.sqrt(2.0 / (n_win * NBINS))
    vmem = pl.BlockSpec(memory_space=pltpu.VMEM)
    out = pl.pallas_call(
        functools.partial(stack_kernel, rows, count // n_chan, scale),
        out_shape=jax.ShapeDtypeStruct((count * GROUPS * n_rec, LANES), f32),
        in_specs=[vmem, vmem, pl.BlockSpec(memory_space=pltpu.SMEM)],
        out_specs=pl.BlockSpec(memory_space=pl.ANY),
        scratch_shapes=[
            pltpu.VMEM((n_win, rows, 2 * NBINS), f32),
            pltpu.VMEM((n_win, n_rec, 16, 2 * NBINS), f32),
            pltpu.VMEM((n_rec * CB, 2 * NBINS), bf16),
            pltpu.VMEM((2 * CB * GROUPS * n_rec, LANES), f32),
            pltpu.SemaphoreType.DMA((2,)),
        ],
        compiler_params=pltpu.CompilerParams(vmem_limit_bytes=40 * 2**20),
        name="stack_correlations",
    )(everything, jnp.asarray(lag_table()), source_rows)
    out = out.reshape(count, GROUPS, n_rec, LANES).transpose(0, 2, 1, 3)
    return out.reshape(count, n_rec, 2 * MAXLAG)


def per_device(records, source_rows):
    n_win, n_chan = lax.axis_size("win"), lax.axis_size("chan")
    _, rows, samples = records.shape
    everything = gathered(records.reshape(rows, samples), n_win, n_chan)
    return stacked(everything, source_rows, rows, n_chan)


def solution(mesh):
    in_specs = (P("win", "chan", None), P())
    out_specs = P(None, ("chan", "win"), None)
    return jax.shard_map(
        per_device, mesh=mesh, in_specs=in_specs, out_specs=out_specs, check_vma=False
    )
```

time: 174 us -> 32.2 us (0.19)
  other arithmetic: 98.3 us -> 0 us
  Pallas kernels: 0 us -> 25.9 us
  local copies, waits for them, and re-layouts: 27 us -> 6.01 us
  blocking collectives: 15.1 us -> 0 us
  matrix products: 14.4 us -> 0 us
  between operations: 13.6 us -> 0.02 us
  starting transfers between devices: 4.97 us -> 0 us
    another operation x6 -> x0, other arithmetic: 95.7 us -> none
    pallas_call x0 -> x2, Pallas kernels: none -> 25.9 us  [the longest x1 15.7 us: gathered(): pl.pallas_call(functools.partial(gather_kernel, n_win, n_chan), out_shape...]
    all_gather x1 -> x0, blocking collectives: 15.1 us -> none  [collect(): portion = lax.all_gather(portion, 'win', axis=0, tiled=True)]
    dot_general x6 -> x0, matrix products: 14.4 us -> none  [the longest x1 6.77 us: transform(): jnp.dot(rounded, weights, preferred_element_type=jnp.float32) * lag_scale]
    reshape x1 -> x0, local copies, waits for them, and re-layouts: 9.75 us -> none  [transform(): return result.reshape(count_src, count_rec, 2 * MAXLAG)]
    gather x2 -> x0, local copies, waits for them, and re-layouts: 7.95 us -> none  [per_device(): source_block = jnp.take(everything, base_rows + chosen_rows, axis=1)]
    all_to_all x1 -> x0, starting transfers between devices: 4.97 us -> none  [per_device(): lax.all_to_all(whitened, 'win', split_axis=1, concat_axis=0, tiled=True)]
    another operation x2 -> x0, local copies, waits for them, and re-layouts: 4.91 us -> none  [the longest x1 4.26 us: cross_terms(): return jnp.stack([real_sum, imag_sum], axis=2)]
  transfers between devices with their start and end apart: 2 -> 0, of which waited for: 0 -> 0; matrix products, arithmetic and copies ran while one was open for 12% -> 0% of each run, Pallas kernels for 0% -> 0%
where the time goes in v1:
time: 32.2 us; the launch traced here: 31.9 us
  Pallas kernels  25.9 us (80%)
  local copies, waits for them, and re-layouts  6.01 us (19%)
    pallas_call x1, Pallas kernels, gathered(): pl.pallas_call(functools.partial(gather_kernel, n_win, n_chan), out_shape...  15.7 us
    pallas_call x1, Pallas kernels, stacked(): pl.pallas_call(functools.partial(stack_kernel, rows, count // n_chan, sca...  10.3 us
    unnamed x10, local copies, waits for them, and re-layouts  6.01 us

profile of v1, /device:TPU:0, one launch (start us, length us, event | category | flops | bytes accessed | tf_op | source)
XLA Modules:
  0.0 31.9 jit_solution(5004567807275890700)
XLA Ops:
  0.0 0.0 copy-start.1
  0.0 1.3 %copy-done.1 = bf16[512,1280]{1,0:T(8,128)(2,1)S(1)} copy-done((bf16[512,1280]{1,0:T(8,128)(2,1)S(1)}, bf16[512,1280]{1,0:T(8,128)(2,1)}, u32[]{:S(2)}) %copy-start.1) | copy-done | bytes 1310744
  1.3 0.0 copy-start.2
  1.3 0.9 %copy-done.2 = bf16[1,16,7680]{2,1,0:T(8,128)(2,1)S(1)} copy-done((bf16[1,16,7680]{2,1,0:T(8,128)(2,1)S(1)}, bf16[1,16,7680]{2,1,0:T(8,128)(2,1)}, u32[]{:S(2)}) %copy-start.2) | copy-done | bytes 245784
  2.3 0.0 copy-start.3
  2.3 0.9 %copy-done.3 = f32[2,15,640]{2,1,0:T(8,128)S(1)} copy-done((f32[2,15,640]{2,1,0:T(8,128)S(1)}, f32[2,15,640]{2,1,0:T(8,128)}, u32[]{:S(2)}) %copy-start.3) | copy-done | bytes 76824
  3.1 15.7 %gather_spectra.1.all_ref = bf16[4,128,1024]{2,1,0:T(8,128)(2,1)S(1)} custom-call(bf16[16,7680]{1,0:T(8,128)(2,1)S(1)} %bitcast.6, bf16[512,1280]{1,0:T(8,128)(2,1)S(1)} %copy-done.1, f32[2,15,640]{2,1,0:T(8,128)S(1)} %copy-done.3), custom_call_target="tpu_custom_call" | custom-call | tf_op jit(solution)/shard_map/gather_spectra/pallas_call | solution.py:160
  18.8 0.0 copy-start
  18.8 2.2 %copy-done = bf16[1024,2048]{1,0:T(8,128)(2,1)S(1)} copy-done((bf16[1024,2048]{1,0:T(8,128)(2,1)S(1)}, bf16[1024,2048]{1,0:T(8,128)(2,1)}, u32[]{:S(2)}) %copy-start) | copy-done | bytes 4194328
  21.0 0.0 copy-start.4
  21.0 0.7 %copy-done.4 = s32[1,256]{1,0:T(1,128)S(1)} copy-done((s32[1,256]{1,0:T(1,128)S(1)}, s32[1,256]{1,0:T(1,128)}, u32[]{:S(2)}) %copy-start.4) | copy-done | bytes 1048
  21.7 10.3 %stack_correlations.1 = f32[16384,128]{1,0:T(8,128)} custom-call(bf16[4,128,1024]{2,1,0:T(8,128)(2,1)S(1)} %gather_spectra.1.all_ref, bf16[1024,2048]{1,0:T(8,128)(2,1)S(1)} %copy-done, s32[1,256]{1,0:T(1,128)S(1)} %copy-done.4), custom_call_target="tpu_custom_call" | custom-call | tf_op jit(solution)/shard_map/stack_correlations/pallas_call | solution.py:256
Async XLA Ops:
  0.0 1.3 %copy-start.1 = (bf16[512,1280]{1,0:T(8,128)(2,1)S(1)}, bf16[512,1280]{1,0:T(8,128)(2,1)}, u32[]{:S(2)}) copy-start(bf16[512,1280]{1,0:T(8,128)(2,1)} %constant.6.clone.table_ref) | copy-start | bytes 3932164
  1.3 0.9 %copy-start.2 = (bf16[1,16,7680]{2,1,0:T(8,128)(2,1)S(1)}, bf16[1,16,7680]{2,1,0:T(8,128)(2,1)}, u32[]{:S(2)}) copy-start(bf16[1,16,7680]{2,1,0:T(8,128)(2,1)} %param.5) | copy-start | bytes 737284
  2.3 0.9 %copy-start.3 = (f32[2,15,640]{2,1,0:T(8,128)S(1)}, f32[2,15,640]{2,1,0:T(8,128)}, u32[]{:S(2)}) copy-start(f32[2,15,640]{2,1,0:T(8,128)} %constant.7.clone.outer_ref) | copy-start | bytes 230404
  18.8 2.2 %copy-start = (bf16[1024,2048]{1,0:T(8,128)(2,1)S(1)}, bf16[1024,2048]{1,0:T(8,128)(2,1)}, u32[]{:S(2)}) copy-start(bf16[1024,2048]{1,0:T(8,128)(2,1)} %constant.8.clone.lag_ref) | copy-start | bytes 12582916
  21.0 0.7 %copy-start.4 = (s32[1,256]{1,0:T(1,128)S(1)}, s32[1,256]{1,0:T(1,128)}, u32[]{:S(2)}) copy-start(s32[1,256]{1,0:T(1,128)} %src_ref.1) | copy-start | bytes 3076

commit v2 on v1

v2 whole, which is shorter than its diff:
```python
import functools
import math

import jax
import jax.numpy as jnp
import ml_dtypes
import numpy as np
from jax import lax
from jax.experimental import pallas as pl
from jax.experimental.pallas import tpu as pltpu
from jax.sharding import PartitionSpec as P

S = 7680
NBINS = 512
HALF = 32
FIRST_BIN = 64
MAXLAG = 1024

INNER = 512
OUTER = S // INNER
LOW = FIRST_BIN - HALF
WIDE = 640
LANES = 128
GROUPS = 2 * MAXLAG // LANES
MESH = pl.DeviceIdType.MESH
bf16 = jnp.bfloat16
f32 = jnp.float32


def angles(left, right):
    turn = np.float32(2.0 * math.pi / S)
    return (left[:, None] * right[None, :] % S).astype(np.float32) * turn


def inner_table():
    a = angles(np.arange(INNER), LOW + np.arange(WIDE))
    return np.concatenate([np.cos(a), -np.sin(a)], axis=1).astype(ml_dtypes.bfloat16)


def outer_table():
    a = angles(INNER * np.arange(OUTER), LOW + np.arange(WIDE))
    return np.stack([np.cos(a), np.sin(a)]).astype(np.float32)


def lag_table():
    a = angles(FIRST_BIN + np.arange(NBINS), np.arange(2 * MAXLAG) - MAXLAG)
    return np.concatenate([np.cos(a), -np.sin(a)], axis=0).astype(ml_dtypes.bfloat16)


def spectra_of(x_ref, table_ref, outer_ref):
    rows = x_ref.shape[0]
    parts = [x_ref[:, i * INNER : (i + 1) * INNER] for i in range(OUTER)]
    z = jnp.dot(
        jnp.concatenate(parts, axis=0), table_ref[...], preferred_element_type=f32
    )
    re = im = None
    for i in range(OUTER):
        zr = z[i * rows : (i + 1) * rows, :WIDE]
        zi = z[i * rows : (i + 1) * rows, WIDE:]
        c = outer_ref[0, i : i + 1, :]
        s = outer_ref[1, i : i + 1, :]
        tr = zr * c + zi * s
        ti = zi * c - zr * s
        re = tr if re is None else re + tr
        im = ti if im is None else im + ti
    return re, im


def whiten(re, im):
    total = jnp.sqrt(re * re + im * im)
    first = total
    span = 1
    while span < 2 * HALF:
        total = total + pltpu.roll(total, WIDE - span, 1)
        span *= 2
    total = total + pltpu.roll(first, WIDE - span, 1)
    amplitude = total[:, :NBINS] / (2 * HALF + 1) + 1e-06
    re = pltpu.roll(re, WIDE - HALF, 1)[:, :NBINS] / amplitude
    im = pltpu.roll(im, WIDE - HALF, 1)[:, :NBINS] / amplitude
    return re.astype(bf16), im.astype(bf16)


def correlate_kernel(
    n_win,
    n_chan,
    rows,
    scale,
    x_hbm,
    table_hbm,
    outer_hbm,
    lag_hbm,
    corr,
    x_ref,
    table_ref,
    outer_ref,
    lag_ref,
    all_ref,
    own,
    wide,
    lhs,
    load,
    s1,
    r1,
    s2,
    r2,
    s3,
    r3,
):
    chips = n_chan // 2
    n_rec = rows // n_win
    lines = GROUPS * n_rec
    per_chip = 2 * rows
    win, chan = lax.axis_index("win"), lax.axis_index("chan")
    chip, core = chan // 2, chan % 2
    sibling = chip * 2 + (1 - core)

    loads = [
        pltpu.make_async_copy(src, dst, load.at[i])
        for i, (src, dst) in enumerate(
            (
                (x_hbm, x_ref),
                (table_hbm, table_ref),
                (outer_hbm, outer_ref),
                (lag_hbm, lag_ref),
            )
        )
    ]
    for c in loads:
        c.start()

    def turn(d):
        return lax.rem(win + d, n_win)

    def peer(p):
        return lax.rem(chip + p, chips) * 2 + core

    barrier = pltpu.get_barrier_semaphore()
    friends = [(chan, turn(d)) for d in range(1, n_win)]
    friends += [(peer(p), win) for p in range(1, chips)] + [(sibling, win)]
    for c, w in friends:
        pl.semaphore_signal(
            barrier, inc=1, device_id={"chan": c, "win": w}, device_id_type=MESH
        )

    for c in loads[:3]:
        c.wait()
    re, im = whiten(*spectra_of(x_ref, table_ref, outer_ref))
    mine = pl.ds(pl.multiple_of(chan * rows, rows), rows)
    all_ref[win, mine, :NBINS] = re
    all_ref[win, mine, NBINS:] = im
    pl.semaphore_wait(barrier, len(friends))

    def copy(w, c, to_c, to_w, send, recv):
        block = all_ref.at[w, pl.ds(pl.multiple_of(c * rows, rows), rows)]
        return pltpu.make_async_remote_copy(
            src_ref=block,
            dst_ref=block,
            send_sem=send,
            recv_sem=recv,
            device_id={"chan": to_c, "win": to_w},
            device_id_type=MESH,
        )

    def along(d):
        return copy(win, chan, chan, turn(d), s1.at[d], r1.at[d])

    def across(d, p):
        return copy(turn(n_win - d), chan, peer(p), win, s2.at[d, p], r2.at[d, p])

    def onward(d, p):
        w, c = turn(n_win - d), peer(chips - p)
        return copy(w, c, sibling, win, s3.at[d, p], r3.at[d, p])

    for d in range(1, n_win):
        along(d).start()
    for d in range(n_win):
        if d:
            copy(turn(n_win - d), chan, chan, turn(d), s1.at[d], r1.at[d]).wait_recv()
        for p in range(1, chips):
            across(d, p).start()
        onward(d, 0).start()

    for w in range(n_win):
        own[w] = all_ref[w, mine, :].astype(f32)
    for w in range(n_win):
        for r in range(n_rec):
            line = own[w, pl.ds(win * n_rec + r, 1), :]
            wide[w, r] = jnp.broadcast_to(line, (16, 2 * NBINS))
    loads[3].wait()

    @pl.loop(1, chips + 1)
    def _(q):
        @pl.when(q < chips)
        def _():
            for d in range(n_win):
                w, c = turn(n_win - d), peer(chips - q)
                copy(w, c, peer(q), win, s2.at[d, q], r2.at[d, q]).wait_recv()
                onward(d, q).start()

        p = q - 1
        there = lax.rem(chip + chips - p, chips)
        for d in range(n_win):
            w, c = turn(n_win - d), there * 2 + (1 - core)
            copy(w, c, sibling, win, s3.at[d, p], r3.at[d, p]).wait_recv()

        for k in range(NBINS // LANES):
            at_re = pl.ds(k * LANES, LANES)
            at_im = pl.ds(NBINS + k * LANES, LANES)

            @pl.loop(0, per_chip // 16)
            def _(i):
                here = pl.ds(pl.multiple_of(there * per_chip + i * 16, 16), 16)
                s_re = [all_ref[w, here, at_re].astype(f32) for w in range(n_win)]
                s_im = [all_ref[w, here, at_im].astype(f32) for w in range(n_win)]
                for r in range(n_rec):
                    re = im = None
                    for w in range(n_win):
                        r_re, r_im = wide[w, r, :, at_re], wide[w, r, :, at_im]
                        a = s_re[w] * r_re + s_im[w] * r_im
                        c = s_im[w] * r_re - s_re[w] * r_im
                        re = a if re is None else re + a
                        im = c if im is None else im + c
                    to = pl.ds(pl.multiple_of(r * per_chip + i * 16, 16), 16)
                    lhs[to, at_re] = re.astype(bf16)
                    lhs[to, at_im] = im.astype(bf16)

        for n in range(GROUPS // 2):
            res = jnp.dot(
                lhs[...], lag_ref[:, n * 256 : (n + 1) * 256], preferred_element_type=f32
            )
            res = res * scale
            for h in range(2):
                for r in range(n_rec):
                    for c in range(0, per_chip, 8):
                        first = (there * per_chip + c) * lines + (2 * n + h) * n_rec + r
                        corr[pl.ds(first, 8, stride=lines), :] = res[
                            r * per_chip + c : r * per_chip + c + 8,
                            h * LANES : (h + 1) * LANES,
                        ]

    for d in range(1, n_win):
        along(d).wait_send()

    @pl.loop(1, chips)
    def _(p):
        for d in range(n_win):
            across(d, p).wait_send()

    @pl.loop(0, chips)
    def _(p):
        for d in range(n_win):
            onward(d, p).wait_send()


def correlated(records, n_win, n_chan):
    rows, samples = records.shape
    chips = n_chan // 2
    n_rec = rows // n_win
    channels = n_chan * rows
    scale = math.sqrt(2.0 / (n_win * NBINS))
    lines = channels * GROUPS * n_rec
    hbm = pl.BlockSpec(memory_space=pltpu.HBM)
    dma = pltpu.SemaphoreType.DMA
    tables = inner_table(), outer_table(), lag_table()
    return pl.pallas_call(
        functools.partial(correlate_kernel, n_win, n_chan, rows, scale),
        out_shape=jax.ShapeDtypeStruct((lines, LANES), f32),
        in_specs=[hbm] * 4,
        out_specs=pl.BlockSpec(memory_space=pltpu.VMEM),
        scratch_shapes=[
            pltpu.VMEM((rows, samples), bf16),
            *[pltpu.VMEM(t.shape, t.dtype) for t in tables],
            pltpu.VMEM((n_win, channels, 2 * NBINS), bf16),
            pltpu.VMEM((n_win, rows, 2 * NBINS), f32),
            pltpu.VMEM((n_win, n_rec, 16, 2 * NBINS), f32),
            pltpu.VMEM((n_rec * 2 * rows, 2 * NBINS), bf16),
            dma((4,)),
            *[dma((n_win,))] * 2,
            *[dma((n_win, chips))] * 4,
        ],
        compiler_params=pltpu.CompilerParams(
            collective_id=0,
            has_side_effects=True,
            vmem_limit_bytes=(20 * 2**20 + lines * LANES * 4),
        ),
        name="correlate_channels",
    )(records, *[jnp.asarray(t) for t in tables])


def spread_kernel(rows, per_shard, lines, corr, src_hbm, out_ref, src_ref, load, sem):
    count = src_ref.shape[1]
    fetch = pltpu.make_async_copy(src_hbm, src_ref, load)
    fetch.start()
    fetch.wait()

    @pl.loop(0, count)
    def _(j):
        c = j // per_shard * rows + src_ref[0, j]
        pltpu.make_async_copy(
            corr.at[pl.ds(pl.multiple_of(c * lines, lines), lines)],
            out_ref.at[pl.ds(pl.multiple_of(j * lines, lines), lines)],
            sem,
        ).start()

    pltpu.make_async_copy(out_ref, out_ref, sem).wait()


def spread(corr, source_rows, rows, n_win, n_chan):
    n_rec = rows // n_win
    count = source_rows.shape[1]
    lines = GROUPS * n_rec
    out = pl.pallas_call(
        functools.partial(spread_kernel, rows, count // n_chan, lines),
        out_shape=jax.ShapeDtypeStruct((count * lines, LANES), f32),
        in_specs=[
            pl.BlockSpec(memory_space=pltpu.VMEM),
            pl.BlockSpec(memory_space=pltpu.HBM),
        ],
        out_specs=pl.BlockSpec(memory_space=pltpu.HBM),
        scratch_shapes=[
            pltpu.SMEM(source_rows.shape, jnp.int32),
            pltpu.SemaphoreType.DMA,
            pltpu.SemaphoreType.DMA,
        ],
        compiler_params=pltpu.CompilerParams(
            vmem_limit_bytes=2**20 + corr.size * 4,
        ),
        name="spread_to_sources",
    )(corr, source_rows)
    out = out.reshape(count, GROUPS, n_rec, LANES).transpose(0, 2, 1, 3)
    return out.reshape(count, n_rec, 2 * MAXLAG)


def per_device(records, source_rows):
    n_win, n_chan = lax.axis_size("win"), lax.axis_size("chan")
    _, rows, samples = records.shape
    corr = correlated(records.reshape(rows, samples), n_win, n_chan)
    return spread(corr, source_rows, rows, n_win, n_chan)


def solution(mesh):
    in_specs = (P("win", "chan", None), P())
    out_specs = P(None, ("chan", "win"), None)
    return jax.shard_map(
        per_device, mesh=mesh, in_specs=in_specs, out_specs=out_specs, check_vma=False
    )
```

time: 32.2 us -> 31.4 us (0.975)
  local copies, waits for them, and re-layouts: 6.01 us -> 5.34 us
    unnamed x10, local copies, waits for them, and re-layouts: 6.01 us -> 5.34 us
where the time goes in v2:
time: 31.4 us; the launch traced here: 31.2 us
  Pallas kernels  25.8 us (82%)
  local copies, waits for them, and re-layouts  5.34 us (17%)
    pallas_call x1, Pallas kernels, correlated(): pl.pallas_call(functools.partial(correlate_kernel, n_win, n_chan, rows, s...  22.1 us
    unnamed x10, local copies, waits for them, and re-layouts  5.34 us
    pallas_call x1, Pallas kernels, spread(): pl.pallas_call(functools.partial(spread_kernel, rows, count // n_chan, li...  3.74 us

profile of v2, /device:TPU:0, one launch (start us, length us, event | category | flops | bytes accessed | tf_op | source)
XLA Modules:
  0.0 31.2 jit_solution(809208084328952643)
XLA Ops:
  0.0 0.0 copy-start
  0.0 2.2 %copy-done = bf16[1024,2048]{1,0:T(8,128)(2,1)S(1)} copy-done((bf16[1024,2048]{1,0:T(8,128)(2,1)S(1)}, bf16[1024,2048]{1,0:T(8,128)(2,1)}, u32[]{:S(2)}) %copy-start) | copy-done | bytes 4194328
  2.2 0.0 copy-start.1
  2.2 1.3 %copy-done.1 = bf16[512,1280]{1,0:T(8,128)(2,1)S(1)} copy-done((bf16[512,1280]{1,0:T(8,128)(2,1)S(1)}, bf16[512,1280]{1,0:T(8,128)(2,1)}, u32[]{:S(2)}) %copy-start.1) | copy-done | bytes 1310744
  3.5 0.0 copy-start.2
  3.5 0.9 %copy-done.2 = bf16[1,16,7680]{2,1,0:T(8,128)(2,1)S(1)} copy-done((bf16[1,16,7680]{2,1,0:T(8,128)(2,1)S(1)}, bf16[1,16,7680]{2,1,0:T(8,128)(2,1)}, u32[]{:S(2)}) %copy-start.2) | copy-done | bytes 245784
  4.5 0.0 copy-start.3
  4.5 0.9 %copy-done.3 = f32[2,15,640]{2,1,0:T(8,128)S(1)} copy-done((f32[2,15,640]{2,1,0:T(8,128)S(1)}, f32[2,15,640]{2,1,0:T(8,128)}, u32[]{:S(2)}) %copy-start.3) | copy-done | bytes 76824
  5.3 0.0 copy-start.4
  5.3 22.1 %correlate_channels.1.corr = f32[8192,128]{1,0:T(8,128)S(1)} custom-call(bf16[16,7680]{1,0:T(8,128)(2,1)S(1)} %bitcast.6, bf16[512,1280]{1,0:T(8,128)(2,1)S(1)} %copy-done.1, f32[2,15,640]{2,1,0:T(8,128)S(1)} %copy-done.3, bf16[1024,2048]{1,0:T(8,128)(2,1)S(1)} %copy-done), custom_call_target="tpu_custom_call" | custom-call | tf_op jit(solution)/shard_map/correlate_channels/pallas_call | solution.py:265
  27.4 0.0 copy-done.4
  27.4 3.7 %spread_to_sources.1 = f32[16384,128]{1,0:T(8,128)} custom-call(f32[8192,128]{1,0:T(8,128)S(1)} %correlate_channels.1.corr, s32[1,256]{1,0:T(1,128)S(1)} %copy-done.4), custom_call_target="tpu_custom_call" | custom-call | tf_op jit(solution)/shard_map/spread_to_sources/pallas_call | solution.py:312
Async XLA Ops:
  0.0 2.2 %copy-start = (bf16[1024,2048]{1,0:T(8,128)(2,1)S(1)}, bf16[1024,2048]{1,0:T(8,128)(2,1)}, u32[]{:S(2)}) copy-start(bf16[1024,2048]{1,0:T(8,128)(2,1)} %constant.8.clone.lag_hbm) | copy-start | bytes 12582916
  2.2 1.3 %copy-start.1 = (bf16[512,1280]{1,0:T(8,128)(2,1)S(1)}, bf16[512,1280]{1,0:T(8,128)(2,1)}, u32[]{:S(2)}) copy-start(bf16[512,1280]{1,0:T(8,128)(2,1)} %constant.6.clone.table_hbm) | copy-start | bytes 3932164
  3.5 0.9 %copy-start.2 = (bf16[1,16,7680]{2,1,0:T(8,128)(2,1)S(1)}, bf16[1,16,7680]{2,1,0:T(8,128)(2,1)}, u32[]{:S(2)}) copy-start(bf16[1,16,7680]{2,1,0:T(8,128)(2,1)} %param.5) | copy-start | bytes 737284
  4.5 0.9 %copy-start.3 = (f32[2,15,640]{2,1,0:T(8,128)S(1)}, f32[2,15,640]{2,1,0:T(8,128)}, u32[]{:S(2)}) copy-start(f32[2,15,640]{2,1,0:T(8,128)} %constant.7.clone.outer_hbm) | copy-start | bytes 230404
  5.3 22.1 %copy-start.4 = (s32[1,256]{1,0:T(1,128)S(1)}, s32[1,256]{1,0:T(1,128)}, u32[]{:S(2)}) copy-start(s32[1,256]{1,0:T(1,128)} %src_hbm.1) | copy-start | bytes 3076

commit v3 on v2

--- a/solution.py
+++ b/solution.py
@@ -131,8 +131,12 @@
     def turn(d):
         return lax.rem(win + d, n_win)
 
+    def other(p):
+        bits = [1 << b for b in range((chips - 1).bit_length())]
+        return sum((chip // b + p // b) % 2 * b for b in bits)
+
     def peer(p):
-        return lax.rem(chip + p, chips) * 2 + core
+        return other(p) * 2 + core
 
     barrier = pltpu.get_barrier_semaphore()
     friends = [(chan, turn(d)) for d in range(1, n_win)]
@@ -168,17 +172,23 @@
         return copy(turn(n_win - d), chan, peer(p), win, s2.at[d, p], r2.at[d, p])
 
     def onward(d, p):
-        w, c = turn(n_win - d), peer(chips - p)
+        w, c = turn(n_win - d), peer(p)
         return copy(w, c, sibling, win, s3.at[d, p], r3.at[d, p])
 
+    near = [p for p in range(1, chips) if p & (p - 1) == 0]
     for d in range(1, n_win):
         along(d).start()
     for d in range(n_win):
         if d:
             copy(turn(n_win - d), chan, chan, turn(d), s1.at[d], r1.at[d]).wait_recv()
         for p in range(1, chips):
-            across(d, p).start()
+            if d == 0 or p in near:
+                across(d, p).start()
         onward(d, 0).start()
+    for d in range(1, n_win):
+        for p in range(1, chips):
+            if p not in near:
+                across(d, p).start()
 
     for w in range(n_win):
         own[w] = all_ref[w, mine, :].astype(f32)
@@ -193,12 +203,12 @@
         @pl.when(q < chips)
         def _():
             for d in range(n_win):
-                w, c = turn(n_win - d), peer(chips - q)
+                w, c = turn(n_win - d), peer(q)
                 copy(w, c, peer(q), win, s2.at[d, q], r2.at[d, q]).wait_recv()
                 onward(d, q).start()
 
         p = q - 1
-        there = lax.rem(chip + chips - p, chips)
+        there = other(p)
         for d in range(n_win):
             w, c = turn(n_win - d), there * 2 + (1 - core)
             copy(w, c, sibling, win, s3.at[d, p], r3.at[d, p]).wait_recv()
@@ -250,6 +260,10 @@
     def _(p):
         for d in range(n_win):
             onward(d, p).wait_send()
+
+
+def in_hbm(array):
+    return pltpu.with_memory_space_constraint(jnp.asarray(array), pltpu.HBM)
 
 
 def correlated(records, n_win, n_chan):
@@ -284,7 +298,7 @@
             vmem_limit_bytes=(20 * 2**20 + lines * LANES * 4),
         ),
         name="correlate_channels",
-    )(records, *[jnp.asarray(t) for t in tables])
+    )(*[in_hbm(t) for t in (records, *tables)])
 
 
 def spread_kernel(rows, per_shard, lines, corr, src_hbm, out_ref, src_ref, load, sem):
@@ -326,7 +340,7 @@
             vmem_limit_bytes=2**20 + corr.size * 4,
         ),
         name="spread_to_sources",
-    )(corr, source_rows)
+    )(corr, in_hbm(source_rows))
     out = out.reshape(count, GROUPS, n_rec, LANES).transpose(0, 2, 1, 3)
     return out.reshape(count, n_rec, 2 * MAXLAG)
 

time: 31.4 us -> 25.2 us (0.80)
  local copies, waits for them, and re-layouts: 5.34 us -> 0 us
  Pallas kernels: 25.8 us -> 25 us
    unnamed x10 -> x0, local copies, waits for them, and re-layouts: 5.34 us -> none
    pallas_call x1, Pallas kernels: 22.1 us -> 21.1 us  [correlated(): pl.pallas_call(functools.partial(correlate_kernel, n_win, n_chan, rows, s...]
where the time goes in v3:
time: 25.2 us; the launch traced here: 25 us
  Pallas kernels  25 us (99%)
    pallas_call x1, Pallas kernels, correlated(): pl.pallas_call(functools.partial(correlate_kernel, n_win, n_chan, rows, s...  21.1 us
    pallas_call x1, Pallas kernels, spread(): pl.pallas_call(functools.partial(spread_kernel, rows, count // n_chan, li...  3.88 us

profile of v3, /device:TPU:0, one launch (start us, length us, event | category | flops | bytes accessed | tf_op | source)
XLA Modules:
  0.0 25.0 jit_solution(2737482336172299907)
XLA Ops:
  0.0 21.1 %correlate_channels.1.corr = f32[8192,128]{1,0:T(8,128)S(1)} custom-call(bf16[16,7680]{1,0:T(8,128)(2,1)} %bitcast.6, bf16[512,1280]{1,0:T(8,128)(2,1)} %constant.6.clone.table_hbm, f32[2,15,640]{2,1,0:T(8,128)} %constant.7.clone.outer_hbm, bf16[1024,2048]{1,0:T(8,128)(2,1)} %constant.8.clone.lag_hbm), custom_call_target="tpu_custom_call" | custom-call | tf_op jit(solution)/shard_map/correlate_channels/pallas_call | solution.py:279
  21.1 3.9 %spread_to_sources.1 = f32[16384,128]{1,0:T(8,128)} custom-call(f32[8192,128]{1,0:T(8,128)S(1)} %correlate_channels.1.corr, s32[1,256]{1,0:T(1,128)} %src_hbm.1), custom_call_target="tpu_custom_call" | custom-call | tf_op jit(solution)/shard_map/spread_to_sources/pallas_call | solution.py:326

commit v4 on v3

--- a/solution.py
+++ b/solution.py
@@ -43,8 +43,8 @@
 
 
 def lag_table():
-    a = angles(FIRST_BIN + np.arange(NBINS), np.arange(2 * MAXLAG) - MAXLAG)
-    return np.concatenate([np.cos(a), -np.sin(a)], axis=0).astype(ml_dtypes.bfloat16)
+    a = angles(FIRST_BIN + np.arange(NBINS), np.arange(MAXLAG + LANES))
+    return np.concatenate([np.cos(a), np.sin(a)], axis=0).astype(ml_dtypes.bfloat16)
 
 
 def spectra_of(x_ref, table_ref, outer_ref):
@@ -234,19 +234,44 @@
                     lhs[to, at_re] = re.astype(bf16)
                     lhs[to, at_im] = im.astype(bf16)
 
-        for n in range(GROUPS // 2):
-            res = jnp.dot(
-                lhs[...], lag_ref[:, n * 256 : (n + 1) * 256], preferred_element_type=f32
+        def at_lags(first, count):
+            at = slice(first, first + count)
+            even = jnp.dot(
+                lhs[:, :NBINS], lag_ref[:NBINS, at], preferred_element_type=f32
             )
-            res = res * scale
-            for h in range(2):
-                for r in range(n_rec):
-                    for c in range(0, per_chip, 8):
-                        first = (there * per_chip + c) * lines + (2 * n + h) * n_rec + r
-                        corr[pl.ds(first, 8, stride=lines), :] = res[
-                            r * per_chip + c : r * per_chip + c + 8,
-                            h * LANES : (h + 1) * LANES,
-                        ]
+            odd = jnp.dot(
+                lhs[:, NBINS:], lag_ref[NBINS:, at], preferred_element_type=f32
+            )
+            return even * scale, odd * scale
+
+        def store(group, block):
+            for r in range(n_rec):
+                for c in range(0, per_chip, 8):
+                    first = (there * per_chip + c) * lines + group * n_rec + r
+                    corr[pl.ds(first, 8, stride=lines), :] = block[
+                        r * per_chip + c : r * per_chip + c + 8
+                    ]
+
+        shape = (n_rec * per_chip, LANES)
+        lane = lax.broadcasted_iota(jnp.int32, shape, 1)
+        mirror = jnp.where(lane == 0, 0, LANES - lane)
+
+        def mirrored(block):
+            return jnp.take_along_axis(block, mirror, axis=1)
+
+        even, odd = at_lags(MAXLAG, LANES)
+        later = mirrored(even + odd)
+        half = GROUPS // 2
+        for n in range(half // 2 - 1, -1, -1):
+            evens, odds = at_lags(n * 256, 256)
+            for h in (1, 0):
+                even = evens[:, h * LANES : (h + 1) * LANES]
+                odd = odds[:, h * LANES : (h + 1) * LANES]
+                group = 2 * n + h
+                store(half + group, even - odd)
+                block = mirrored(even + odd)
+                store(half - 1 - group, jnp.where(lane == 0, later, block))
+                later = block
 
     for d in range(1, n_win):
         along(d).wait_send()
@@ -307,7 +332,7 @@
     fetch.start()
     fetch.wait()
 
-    @pl.loop(0, count)
+    @pl.loop(0, count, unroll=8)
     def _(j):
         c = j // per_shard * rows + src_ref[0, j]
         pltpu.make_async_copy(
@@ -340,7 +365,7 @@
             vmem_limit_bytes=2**20 + corr.size * 4,
         ),
         name="spread_to_sources",
-    )(corr, in_hbm(source_rows))
+    )(corr, source_rows)
     out = out.reshape(count, GROUPS, n_rec, LANES).transpose(0, 2, 1, 3)
     return out.reshape(count, n_rec, 2 * MAXLAG)
 

time: 25.2 us -> 24.4 us (0.968)
  Pallas kernels: 25 us -> 24.2 us
    pallas_call x1, Pallas kernels: 21.1 us -> 20.5 us  [correlated(): pl.pallas_call(functools.partial(correlate_kernel, n_win, n_chan, rows, s...]
where the time goes in v4:
time: 24.4 us; the launch traced here: 24.2 us
  Pallas kernels  24.2 us (99%)
    pallas_call x1, Pallas kernels, correlated(): pl.pallas_call(functools.partial(correlate_kernel, n_win, n_chan, rows, s...  20.5 us
    pallas_call x1, Pallas kernels, spread(): pl.pallas_call(functools.partial(spread_kernel, rows, count // n_chan, li...  3.74 us

profile of v4, /device:TPU:0, one launch (start us, length us, event | category | flops | bytes accessed | tf_op | source)
XLA Modules:
  0.0 24.2 jit_solution(513853095563838425)
XLA Ops:
  0.0 0.0 copy-start
  0.0 20.5 %correlate_channels.1.corr = f32[8192,128]{1,0:T(8,128)S(1)} custom-call(bf16[16,7680]{1,0:T(8,128)(2,1)} %bitcast.6, bf16[512,1280]{1,0:T(8,128)(2,1)} %constant.6.clone.table_hbm, f32[2,15,640]{2,1,0:T(8,128)} %constant.7.clone.outer_hbm, bf16[1024,1152]{1,0:T(8,128)(2,1)} %constant.8.clone.lag_hbm), custom_call_target="tpu_custom_call" | custom-call | tf_op jit(solution)/shard_map/correlate_channels/pallas_call | solution.py:304
  20.5 0.0 copy-done
  20.5 3.7 %spread_to_sources.1 = f32[16384,128]{1,0:T(8,128)} custom-call(f32[8192,128]{1,0:T(8,128)S(1)} %correlate_channels.1.corr, s32[1,256]{1,0:T(1,128)S(1)} %copy-done), custom_call_target="tpu_custom_call" | custom-call | tf_op jit(solution)/shard_map/spread_to_sources/pallas_call | solution.py:351
Async XLA Ops:
  0.0 20.5 %copy-start = (s32[1,256]{1,0:T(1,128)S(1)}, s32[1,256]{1,0:T(1,128)}, u32[]{:S(2)}) copy-start(s32[1,256]{1,0:T(1,128)} %src_hbm.1) | copy-start | bytes 3076
